TPU v7x, 256 devices: a whole 4x4x8 slice. The times are simulated.
256 devices in a mesh: leaf: 4 (over y), row: 16 (over z, x_lo), col: 4 (over x_hi, core).
Axes of the slice: x: 4 (x_hi: 2, x_lo: 2; x = x_hi * 2 + x_lo), y: 4, z: 8, core: 2. Of those that a mesh axis runs over, the one named last changes fastest.
Arguments:
- rhs_top: float32 [8192, 64], P(('leaf', 'row')), may hold values from -6 to 6
- rhs_mid: float32 [8192, 64], P(('leaf', 'row')), may hold values from -6 to 6
- rhs_low: float32 [8192, 64], P(('leaf', 'row')), may hold values from -6 to 6
- inverse_top: float32 [8192, 8192], P(('leaf', 'row'), 'col'), as said below
- inverse_mid: float32 [8192, 4096], P(('leaf', 'row'), 'col'), as said below
- inverse_low: float32 [8192, 2048], P(('leaf', 'row'), 'col'), as said below
- tiles_mid: float32 [4, 16, 4, 4, 128, 128], P('leaf', 'row', 'col'), may hold values from -0.25 to 0.25
- places_mid: int32 [4, 16, 4, 4], P('leaf', 'row', 'col'), may hold values from 0 to 15, as said below
- tiles_low: float32 [4, 16, 4, 2, 128, 128], P('leaf', 'row', 'col'), may hold values from -0.375 to 0.375
- places_low: int32 [4, 16, 4, 2], P('leaf', 'row', 'col'), may hold values from 0 to 7, as said below
Outputs:
- solved_top: float32 [8192, 64], P(('leaf', 'row'))
- solved_mid: float32 [8192, 64], P(('leaf', 'row'))
- solved_low: float32 [8192, 64], P(('leaf', 'row'))
Inputs may be any that keep to these rules, and one draw needn't show every extreme that they name: `places_mid`: within one device the 4 positions are distinct, a quarter of the device's (16) x (1) tile slots. `places_low`: within one device the 2 positions are distinct, a quarter of the device's (8) x (1) tile slots. `inverse_top`: each separator's square block is lower triangular with positive diagonal. `inverse_mid`: each separator's square block is lower triangular with positive diagonal. `inverse_low`: each separator's square block is lower triangular with positive diagonal.
All inputs are finite; a program needn't handle non-finite values.
Results may differ from a plain program's by a relative error of at most 0.00014.
Values sent between devices are 32-bit elements; how exact they have to be, the bound alone decides.
A program may use at most 64 MiB of HBM per device.

v0:
```python
import jax
import jax.numpy as jnp
from jax import lax
from jax.sharding import PartitionSpec as P

highest = lax.Precision.HIGHEST


def partner(block, axis, apart):
    count = lax.axis_size(axis)
    route = []
    for low in range(count):
        high = low | 1 << apart
        if high != low and high < count:
            route += [(low, high), (high, low)]
    return lax.ppermute(block, axis, route)


def group_total(part, leaf_bits_used):
    col_size, vec_width = part.shape
    folded = part.reshape(col_size // 2, 2 * vec_width)
    share_part = lax.psum_scatter(folded, "row", scatter_dimension=0, tiled=True)
    for bit_index in range(leaf_bits_used):
        share_part = share_part + partner(share_part, "leaf", bit_index)
    summed = lax.all_gather(share_part, "row", axis=0, tiled=True)
    return summed.reshape(col_size, vec_width)


def col_total(part):
    return lax.psum(part, "col")


def col_pair(first_part, second_part):
    return lax.psum((first_part, second_part), "col")


def into_columns(own_vec, shift, col_size):
    own_count, vec_width = own_vec.shape
    padded = jnp.zeros((col_size + 2 * own_count, vec_width), jnp.float32)
    begin_at = jnp.clip(shift + own_count, 0, col_size + own_count)
    placed = lax.dynamic_update_slice_in_dim(padded, own_vec, begin_at, 0)
    return placed[own_count : own_count + col_size]


def from_columns(columns, shift, own_count):
    col_size = columns.shape[0]
    padded = jnp.pad(columns, ((own_count, own_count), (0, 0)))
    begin_at = jnp.clip(shift + own_count, 0, col_size + own_count)
    return lax.dynamic_slice_in_dim(padded, begin_at, own_count, 0)


def forward(inverse, columns):
    return jnp.dot(inverse, columns, precision=highest, preferred_element_type=jnp.float32)


def backward(inverse, own_vec):
    return lax.dot_general(
        inverse,
        own_vec,
        (((0,), (0,)), ((), ())),
        precision=highest,
        preferred_element_type=jnp.float32,
    )


def lift_tiles(tile_set, places, child_vec, col_size):
    tile_count = places.shape[-1]
    tile_size = tile_set.shape[-1]
    per_row = child_vec.shape[0] // tile_size
    squares = tile_set.reshape(tile_count, tile_size, tile_size)
    positions = places.reshape(tile_count)
    tile_row = positions // per_row
    tile_col = positions % per_row
    pieces = child_vec.reshape(per_row, tile_size, -1)[tile_col]
    product = jnp.einsum("nab,nbw->naw", squares, pieces, precision=highest)
    chooser = (
        jnp.arange(col_size // tile_size, dtype=jnp.int32)[:, None] == tile_row[None, :]
    ).astype(jnp.float32)
    return jnp.einsum("kn,naw->kaw", chooser, product, precision=highest).reshape(col_size, -1)


def lower_tiles(tile_set, places, parent_cols, own_count):
    tile_count = places.shape[-1]
    tile_size = tile_set.shape[-1]
    per_row = own_count // tile_size
    squares = tile_set.reshape(tile_count, tile_size, tile_size)
    positions = places.reshape(tile_count)
    tile_row = positions // per_row
    tile_col = positions % per_row
    pieces = parent_cols.reshape(parent_cols.shape[0] // tile_size, tile_size, -1)[tile_row]
    product = jnp.einsum("nba,nbw->naw", squares, pieces, precision=highest)
    chooser = (jnp.arange(per_row, dtype=jnp.int32)[:, None] == tile_col[None, :]).astype(
        jnp.float32
    )
    return jnp.einsum("kn,naw->kaw", chooser, product, precision=highest).reshape(own_count, -1)


def body(
    rhs_top,
    rhs_mid,
    rhs_low,
    inverse_top,
    inverse_mid,
    inverse_low,
    tiles_mid,
    places_mid,
    tiles_low,
    places_low,
):
    own_count = rhs_top.shape[0]
    leaf_count = lax.axis_size("leaf")
    leaf_bits = leaf_count.bit_length() - 1
    row_count = lax.axis_size("row")
    leaf_index = lax.axis_index("leaf")
    row_index = lax.axis_index("row")
    col_index = lax.axis_index("col")

    def placing(depth_level, col_size):
        leaf_span = leaf_count >> depth_level
        v_offset = (leaf_index % leaf_span * row_count + row_index) * own_count
        return v_offset - col_index * col_size

    size_top = inverse_top.shape[1]
    size_mid = inverse_mid.shape[1]
    size_low = inverse_low.shape[1]
    shift_top = placing(0, size_top)
    shift_mid = placing(1, size_mid)
    shift_low = placing(2, size_low)
    bits_mid = leaf_bits - 1
    bits_low = leaf_bits - 2
    base_low = group_total(into_columns(rhs_low, shift_low, size_low), bits_low)
    base_mid = group_total(into_columns(rhs_mid, shift_mid, size_mid), bits_mid)
    base_top = group_total(into_columns(rhs_top, shift_top, size_top), leaf_bits)
    low_y = col_total(forward(inverse_low, base_low))
    mid_cols = base_mid - group_total(lift_tiles(tiles_low, places_low, low_y, size_mid), bits_mid)
    mid_y = col_total(forward(inverse_mid, mid_cols))
    top_cols = base_top - group_total(lift_tiles(tiles_mid, places_mid, mid_y, size_top), leaf_bits)
    top_y = col_total(forward(inverse_top, top_cols))
    back_top = group_total(backward(inverse_top, top_y), leaf_bits)
    solved_top, down_mid = col_pair(
        from_columns(back_top, shift_top, own_count),
        lower_tiles(tiles_mid, places_mid, back_top, own_count),
    )
    back_mid = group_total(backward(inverse_mid, mid_y - down_mid), bits_mid)
    solved_mid, down_low = col_pair(
        from_columns(back_mid, shift_mid, own_count),
        lower_tiles(tiles_low, places_low, back_mid, own_count),
    )
    back_low = group_total(backward(inverse_low, low_y - down_low), bits_low)
    solved_low = col_total(from_columns(back_low, shift_low, own_count))
    return (solved_top, solved_mid, solved_low)


def solution(mesh):
    return jax.shard_map(
        body,
        mesh=mesh,
        in_specs=(
            P(("leaf", "row"), None),
            P(("leaf", "row"), None),
            P(("leaf", "row"), None),
            P(("leaf", "row"), "col"),
            P(("leaf", "row"), "col"),
            P(("leaf", "row"), "col"),
            P("leaf", "row", "col", None, None, None),
            P("leaf", "row", "col", None),
            P("leaf", "row", "col", None, None, None),
            P("leaf", "row", "col", None),
        ),
        out_specs=(P(("leaf", "row"), None), P(("leaf", "row"), None), P(("leaf", "row"), None)),
        check_vma=False,
    )
```

profile of v0, /device:TPU:1, one launch (start us, length us, event | category | flops | bytes accessed | tf_op | source)
XLA Modules:
  0.0 885.7 jit_solution(1058798755863715967)
XLA Ops:
  11.3 60.5 %reduce-scatter.13.cloned.1.call-done = f32[16,128]{1,0:T(8,128)} async-done(((f32[256,128]{1,0:T(8,128)}), f32[16,128]{1,0:T(8,128)}) %reduce-scatter.13.cloned.1.call-update) | async-done | bytes 8208 | tf_op jit(solution)/shard_map/reduce_scatter | solution.py:22
  71.8 24.7 %all_gather.26 = f32[256,128]{1,0:T(8,128)S(1)} all-gather(f32[16,128]{1,0:T(8,128)} %reduce-scatter.13.cloned.1.call-done), channel_id=1, replica_groups=mesh['leaf'=4,'row'=16,'col'=4] {'row'}, dimensions={0}, use_global_device_ids=true | all-gather | bytes 139264 | tf_op jit(solution)/shard_map/all_gather | solution.py:25
  97.2 32.0 %psum.56 = f32[128,64]{0,1:T(8,128)S(1)} all-reduce(f32[128,64]{0,1:T(8,128)S(1)} %convolution_bitcast_fusion.7), channel_id=1, replica_groups=mesh['leaf'=4,'row'=16,'col'=4] {'col'}, use_global_device_ids=true, to_apply=%region_3.4 | all-reduce | flops 8192 | bytes 65536 | tf_op jit(solution)/shard_map/psum | solution.py:30
  133.3 10.0 %reduce-scatter.11.cloned.1.call-done = f32[32,128]{1,0:T(8,128)} async-done(((f32[512,128]{1,0:T(8,128)}), f32[32,128]{1,0:T(8,128)}) %reduce-scatter.11.cloned.1.call-update) | async-done | bytes 16400 | tf_op jit(solution)/shard_map/reduce_scatter | solution.py:22
  147.2 66.3 %reduce-scatter.15.cloned.1.call-done = f32[32,128]{1,0:T(8,128)} async-done(((f32[512,128]{1,0:T(8,128)}), f32[32,128]{1,0:T(8,128)}) %reduce-scatter.15.cloned.1.call-update) | async-done | bytes 16400 | tf_op jit(solution)/shard_map/reduce_scatter | solution.py:22
  214.5 25.0 %all_gather.25 = f32[512,128]{1,0:T(8,128)S(1)} all-gather(f32[32,128]{1,0:T(8,128)S(1)} %add.158), channel_id=1, replica_groups=mesh['leaf'=4,'row'=16,'col'=4] {'row'}, dimensions={0}, use_global_device_ids=true | all-gather | bytes 278528 | tf_op jit(solution)/shard_map/all_gather | solution.py:25
  240.2 26.5 %all_gather.27 = f32[512,128]{1,0:T(8,128)S(1)} all-gather(f32[32,128]{1,0:T(8,128)S(1)} %add.160), channel_id=1, replica_groups=mesh['leaf'=4,'row'=16,'col'=4] {'row'}, dimensions={0}, use_global_device_ids=true | all-gather | bytes 278528 | tf_op jit(solution)/shard_map/all_gather | solution.py:25
  268.0 37.9 %psum.57 = f32[128,64]{0,1:T(8,128)S(1)} all-reduce(f32[128,64]{0,1:T(8,128)S(1)} %convolution_bitcast_fusion.6), channel_id=1, replica_groups=mesh['leaf'=4,'row'=16,'col'=4] {'col'}, use_global_device_ids=true, to_apply=%region_5.6 | all-reduce | flops 8192 | bytes 65536 | tf_op jit(solution)/shard_map/psum | solution.py:30
  312.4 2.8 collective-permute-start.1
  315.3 52.2 %reduce-scatter.17.cloned.1.call-done = f32[64,128]{1,0:T(8,128)} async-done(((f32[1024,128]{1,0:T(8,128)}), f32[64,128]{1,0:T(8,128)}) %reduce-scatter.17.cloned.1.call-update) | async-done | bytes 32784 | tf_op jit(solution)/shard_map/reduce_scatter | solution.py:22
  371.6 2.7 collective-permute-start.5
  374.3 26.6 %all_gather.24 = f32[1024,128]{1,0:T(8,128)S(1)} all-gather(f32[64,128]{1,0:T(8,128)S(1)} %add.154), channel_id=1, replica_groups=mesh['leaf'=4,'row'=16,'col'=4] {'row'}, dimensions={0}, use_global_device_ids=true | all-gather | bytes 557056 | tf_op jit(solution)/shard_map/all_gather | solution.py:25
  400.9 27.0 %all_gather.28 = f32[1024,128]{1,0:T(8,128)S(1)} all-gather(f32[64,128]{1,0:T(8,128)S(1)} %add.162), channel_id=1, replica_groups=mesh['leaf'=4,'row'=16,'col'=4] {'row'}, dimensions={0}, use_global_device_ids=true | all-gather | bytes 557056 | tf_op jit(solution)/shard_map/all_gather | solution.py:25
  430.0 40.2 %psum.58 = f32[128,64]{0,1:T(8,128)S(1)} all-reduce(f32[128,64]{0,1:T(8,128)S(1)} %convolution_bitcast_fusion.5), channel_id=1, replica_groups=mesh['leaf'=4,'row'=16,'col'=4] {'col'}, use_global_device_ids=true, to_apply=%region_7.8 | all-reduce | flops 8192 | bytes 65536 | tf_op jit(solution)/shard_map/psum | solution.py:30
  472.3 56.4 %reduce-scatter.19.cloned.1.call-done = f32[64,128]{1,0:T(8,128)} async-done(((f32[1024,128]{1,0:T(8,128)}), f32[64,128]{1,0:T(8,128)}) %reduce-scatter.19.cloned.1.call-update) | async-done | bytes 32784 | tf_op jit(solution)/shard_map/reduce_scatter | solution.py:22
  532.8 2.7 collective-permute-start.7
  537.1 26.5 %all_gather.29 = f32[1024,128]{1,0:T(8,128)S(1)} all-gather(f32[64,128]{1,0:T(8,128)S(1)} %add.164), channel_id=1, replica_groups=mesh['leaf'=4,'row'=16,'col'=4] {'row'}, dimensions={0}, use_global_device_ids=true | all-gather | bytes 557056 | tf_op jit(solution)/shard_map/all_gather | solution.py:25
  567.0 33.4 %psum.60 = f32[128,64]{0,1:T(8,128)S(1)} all-reduce(f32[128,64]{0,1:T(8,128)S(1)} %bitcast.66), channel_id=1, replica_groups=mesh['leaf'=4,'row'=16,'col'=4] {'col'}, use_global_device_ids=true, to_apply=%region_10.11 | all-reduce | flops 8192 | bytes 65536 | tf_op jit(solution)/shard_map/psum | solution.py:34
  602.7 58.2 %reduce-scatter.21.cloned.1.call-done = f32[32,128]{1,0:T(8,128)} async-done(((f32[512,128]{1,0:T(8,128)}), f32[32,128]{1,0:T(8,128)}) %reduce-scatter.21.cloned.1.call-update) | async-done | bytes 16400 | tf_op jit(solution)/shard_map/reduce_scatter | solution.py:22
  664.9 25.6 %all_gather.30 = f32[512,128]{1,0:T(8,128)S(1)} all-gather(f32[32,128]{1,0:T(8,128)S(1)} %add.166), channel_id=1, replica_groups=mesh['leaf'=4,'row'=16,'col'=4] {'row'}, dimensions={0}, use_global_device_ids=true | all-gather | bytes 278528 | tf_op jit(solution)/shard_map/all_gather | solution.py:25
  691.8 32.3 %psum.62 = f32[128,64]{0,1:T(8,128)S(1)} all-reduce(f32[128,64]{0,1:T(8,128)S(1)} %bitcast.67), channel_id=1, replica_groups=mesh['leaf'=4,'row'=16,'col'=4] {'col'}, use_global_device_ids=true, to_apply=%region_13.14 | all-reduce | flops 8192 | bytes 65536 | tf_op jit(solution)/shard_map/psum | solution.py:34
  727.0 56.7 %reduce-scatter.23.cloned.1.call-done = f32[16,128]{1,0:T(8,128)} async-done(((f32[256,128]{1,0:T(8,128)}), f32[16,128]{1,0:T(8,128)}) %reduce-scatter.23.cloned.1.call-update) | async-done | bytes 8208 | tf_op jit(solution)/shard_map/reduce_scatter | solution.py:22
  783.7 24.6 %all_gather.31 = f32[256,128]{1,0:T(8,128)S(1)} all-gather(f32[16,128]{1,0:T(8,128)} %reduce-scatter.23.cloned.1.call-done), channel_id=1, replica_groups=mesh['leaf'=4,'row'=16,'col'=4] {'row'}, dimensions={0}, use_global_device_ids=true | all-gather | bytes 139264 | tf_op jit(solution)/shard_map/all_gather | solution.py:25
  809.0 65.5 %all-reduce.6.cloned.1.call-done = (f32[128,64]{1,0:T(8,128)}, f32[128,64]{1,0:T(8,128)}, f32[128,64]{1,0:T(8,128)}) async-done(((f32[128,64]{1,0:T(8,128)}, f32[128,64]{1,0:T(8,128)}, f32[128,64]{1,0:T(8,128)}), (f32[128,64]{1,0:T(8,128)}, f32[128,64]{1,0:T(8,128)}, f32[128,64]{1,0:T(8,128)})) %all-reduce.6.cloned.1.call-update) | async-done | bytes 98320 | tf_op jit(solution)/shard_map/psum | solution.py:34
  (132 shorter events, 55.1 us)
Async XLA Ops:
  7.2 421.0 %copy-start = (f32[128,2048]{1,0:T(8,128)S(1)}, f32[128,2048]{1,0:T(8,128)}, u32[]{:S(2)}) copy-start(f32[128,2048]{1,0:T(8,128)} %param.13) | copy-start | bytes 3145732
  7.2 64.7 %reduce-scatter.13.cloned.1.call-start = ((), (), s32[]{:S(2)}) async-start(), calls=%async_computation.10 | async-start | bytes 139264 | tf_op jit(solution)/shard_map/reduce_scatter | solution.py:22
  9.5 133.7 %reduce-scatter.11.cloned.1.call-start = ((), (), s32[]{:S(2)}) async-start(), calls=%async_computation.9 | async-start | bytes 278528 | tf_op jit(solution)/shard_map/reduce_scatter | solution.py:22
  10.4 118.9 %copy-start.5 = (f32[1,1,1,2,128,128]{5,4,3,2,1,0:T(8,128)S(1)}, f32[1,1,1,2,128,128]{5,4,3,2,1,0:T(8,128)}, u32[]{:S(2)}) copy-start(f32[1,1,1,2,128,128]{5,4,3,2,1,0:T(8,128)} %param.18) | copy-start | bytes 393220
  10.4 119.4 %copy-start.11 = (s32[1,1,1,2]{3,2,1,0:T(1,128)S(1)}, s32[1,1,1,2]{3,2,1,0:T(1,128)}, u32[]{:S(2)}) copy-start(s32[1,1,1,2]{3,2,1,0:T(1,128)} %param.19) | copy-start | bytes 28
  11.3 202.2 %reduce-scatter.15.cloned.1.call-start = ((), (), s32[]{:S(2)}) async-start(), calls=%async_computation.11 | async-start | bytes 278528 | tf_op jit(solution)/shard_map/reduce_scatter | solution.py:22
  131.3 177.3 %reduce-scatter.9.cloned.1.call-start = ((), (), s32[]{:S(2)}) async-start(), calls=%async_computation.8 | async-start | bytes 557056 | tf_op jit(solution)/shard_map/reduce_scatter | solution.py:22
  133.2 133.7 %copy-start.1 = (f32[128,1024]{1,0:T(8,128)S(1)}, f32[128,1024]{1,0:T(8,128)}, u32[]{:S(2)}) copy-start(f32[128,1024]{1,0:T(8,128)} %param.14) | copy-start | bytes 1572868
  133.2 234.2 %reduce-scatter.17.cloned.1.call-start = ((), (), s32[]{:S(2)}) async-start(), calls=%async_computation.12 | async-start | bytes 557056 | tf_op jit(solution)/shard_map/reduce_scatter | solution.py:22
  143.2 3.2 collective-permute-start.2
  213.5 26.0 %collective-permute-start.3 = (f32[32,128]{1,0:T(8,128)}, f32[32,128]{1,0:T(8,128)S(1)}, u32[]{:S(2)}, u32[]{:S(2)}) collective-permute-start(f32[32,128]{1,0:T(8,128)} %reduce-scatter.15.cloned.1.call-done), channel_id=1, source_target_pairs={{0,64},{64,0},{128,192},{192,128},{1,65},{65,1},{129,193},{193,129... | collective-permute-start | bytes 49160 | tf_op jit(solution)/shard_map/ppermute | solution.py:16
  308.5 220.1 %reduce-scatter.19.cloned.1.call-start = ((), (), s32[]{:S(2)}) async-start(), calls=%async_computation.13 | async-start | bytes 557056 | tf_op jit(solution)/shard_map/reduce_scatter | solution.py:22
  308.6 3.1 collective-permute-start
  312.4 56.2 %collective-permute-start.1 = (f32[64,128]{1,0:T(8,128)S(1)}, f32[64,128]{1,0:T(8,128)S(1)}, u32[]{:S(2)}, u32[]{:S(2)}) collective-permute-start(f32[64,128]{1,0:T(8,128)S(1)} %add.153), channel_id=1, source_target_pairs={{0,128},{128,0},{64,192},{192,64},{1,129},{129,1},{65,193},{193,65... | collective-permute-start | bytes 98312 | tf_op jit(solution)/shard_map/ppermute | solution.py:16
  367.4 3.4 collective-permute-start.4
  371.6 29.3 %collective-permute-start.5 = (f32[64,128]{1,0:T(8,128)S(1)}, f32[64,128]{1,0:T(8,128)S(1)}, u32[]{:S(2)}, u32[]{:S(2)}) collective-permute-start(f32[64,128]{1,0:T(8,128)S(1)} %add.161), channel_id=1, source_target_pairs={{0,128},{128,0},{64,192},{192,64},{1,129},{129,1},{65,193},{193,65... | collective-permute-start | bytes 98312 | tf_op jit(solution)/shard_map/ppermute | solution.py:16
  472.2 188.7 %reduce-scatter.21.cloned.1.call-start = ((), (), s32[]{:S(2)}) async-start(), calls=%async_computation.14 | async-start | bytes 278528 | tf_op jit(solution)/shard_map/reduce_scatter | solution.py:22
  528.7 3.4 collective-permute-start.6
  532.8 4.3 collective-permute-start.7
  602.6 121.5 %copy-start.4 = (f32[128,512]{1,0:T(8,128)S(1)}, f32[128,512]{1,0:T(8,128)}, u32[]{:S(2)}) copy-start(f32[128,512]{1,0:T(8,128)} %param.15) | copy-start | bytes 786436
  602.6 121.5 %copy-start.7 = (f32[128,64]{0,1:T(8,128)S(1)}, f32[128,64]{0,1:T(8,128)}, u32[]{:S(2)}) copy-start(f32[128,64]{0,1:T(8,128)} %copy-done.6) | copy-start | bytes 98308
  602.6 181.1 %reduce-scatter.23.cloned.1.call-start = ((), (), s32[]{:S(2)}) async-start(), calls=%async_computation.15 | async-start | bytes 139264 | tf_op jit(solution)/shard_map/reduce_scatter | solution.py:22
  660.9 3.2 collective-permute-start.8
  725.2 149.3 %all-reduce.6.cloned.1.call-start = ((), (), s32[]{:S(2)}) async-start(), calls=%async_computation.16 | async-start | bytes 393216 | tf_op jit(solution)/shard_map/psum | solution.py:34
  (7 other events, 171.2 us)
Sparse Core Ops, SparseCore 0:
  10.5 61.2 reduce-scatter.12
  74.5 68.7 reduce-scatter.10
  145.7 67.6 reduce-scatter.14
  216.0 69.3 reduce-scatter.8
  308.7 58.7 reduce-scatter.16
  472.3 56.3 reduce-scatter.18
  602.8 58.1 reduce-scatter.20
  725.4 58.2 reduce-scatter.22
  809.2 65.3 all-reduce.5
where the time goes:
time: 887 us; the launch traced here: 886 us
  waiting for transfers between devices  438 us (49%)
  blocking collectives  382 us (43%)
  local copies, waits for them, and re-layouts  21.3 us (2%)
  starting transfers between devices  15.7 us (2%)
  between operations  14.4 us (2%)
  matrix products  9.91 us (1%)
    reduce_scatter x8, waiting for transfers between devices, group_total(): lax.psum_scatter(folded, 'row', scatter_dimension=0, tiled=True)  360 us
    all_gather x8, blocking collectives, group_total(): summed = lax.all_gather(share_part, 'row', axis=0, tiled=True)  206 us
    psum x3, blocking collectives, col_total(): return lax.psum(part, 'col')  110 us
    psum x2, blocking collectives, col_pair(): return lax.psum((first_part, second_part), 'col')  65.7 us
    psum x1, waiting for transfers between devices, col_pair(): return lax.psum((first_part, second_part), 'col')  65.5 us
  transfers between devices with their start and end apart: 18, of which 14 were waited for; matrix products, arithmetic and copies ran while one was open for 2% of the time, Pallas kernels for 0%

commit v1 on v0

--- a/solution.py
+++ b/solution.py
@@ -22,7 +22,10 @@
     share_part = lax.psum_scatter(folded, "row", scatter_dimension=0, tiled=True)
     for bit_index in range(leaf_bits_used):
         share_part = share_part + partner(share_part, "leaf", bit_index)
-    summed = lax.all_gather(share_part, "row", axis=0, tiled=True)
+    current_block = jax.lax.axis_size("row")
+    f_now = jnp.stack([share_part] * current_block)
+    y = jax.lax.all_to_all(f_now, "row", 0, 0)
+    summed = jnp.concatenate(y, axis=0)
     return summed.reshape(col_size, vec_width)
 
 

time: 887 us -> 794 us (0.90)
  blocking collectives: 382 us -> 154 us
  waiting for transfers between devices: 438 us -> 532 us
  starting transfers between devices: 15.7 us -> 49 us
    all_gather x8 -> x0, blocking collectives: 206 us -> none  [group_total(): summed = lax.all_gather(share_part, 'row', axis=0, tiled=True)]
    reduce_scatter x8, waiting for transfers between devices: 360 us -> 417 us  [group_total(): lax.psum_scatter(folded, 'row', scatter_dimension=0, tiled=True)]
    all_to_all x0 -> x7, waiting for transfers between devices: none -> 42.3 us  [group_total(): y = jax.lax.all_to_all(f_now, 'row', 0, 0)]
    all_to_all x0 -> x7, starting transfers between devices: none -> 32.3 us  [group_total(): y = jax.lax.all_to_all(f_now, 'row', 0, 0)]
    psum x3, blocking collectives: 110 us -> 81.8 us  [col_total(): return lax.psum(part, 'col')]
    all_to_all x0 -> x1, blocking collectives: none -> 17 us  [group_total(): y = jax.lax.all_to_all(f_now, 'row', 0, 0)]
    psum x2, blocking collectives: 65.7 us -> 55.4 us  [col_pair(): return lax.psum((first_part, second_part), 'col')]
    psum x1, waiting for transfers between devices: 65.5 us -> 55.7 us  [col_pair(): return lax.psum((first_part, second_part), 'col')]
  transfers between devices with their start and end apart: 18 -> 25, of which waited for: 14 -> 23; matrix products, arithmetic and copies ran while one was open for 2% -> 2% of each run, Pallas kernels for 0% -> 0%
where the time goes in v1:
time: 794 us; the launch traced here: 792 us
  waiting for transfers between devices  532 us (67%)
  blocking collectives  154 us (19%)
  starting transfers between devices  49 us (6%)
  local copies, waits for them, and re-layouts  27.9 us (4%)
  between operations  14.5 us (2%)
  matrix products  9.15 us (1%)
    reduce_scatter x8, waiting for transfers between devices, group_total(): lax.psum_scatter(folded, 'row', scatter_dimension=0, tiled=True)  417 us
    psum x3, blocking collectives, col_total(): return lax.psum(part, 'col')  81.8 us
    psum x1, waiting for transfers between devices, col_pair(): return lax.psum((first_part, second_part), 'col')  55.7 us
    psum x2, blocking collectives, col_pair(): return lax.psum((first_part, second_part), 'col')  55.4 us
    all_to_all x7, waiting for transfers between devices, group_total(): y = jax.lax.all_to_all(f_now, 'row', 0, 0)  42.3 us
    all_to_all x7, starting transfers between devices, group_total(): y = jax.lax.all_to_all(f_now, 'row', 0, 0)  32.3 us
    ppermute x9, waiting for transfers between devices, partner(): return lax.ppermute(block, axis, route)  17.5 us
    all_to_all x1, blocking collectives, group_total(): y = jax.lax.all_to_all(f_now, 'row', 0, 0)  17 us
  transfers between devices with their start and end apart: 25, of which 23 were waited for; matrix products, arithmetic and copies ran while one was open for 2% of the time, Pallas kernels for 0%

profile of v1, /device:TPU:1, one launch (start us, length us, event | category | flops | bytes accessed | tf_op | source)
XLA Modules:
  0.0 792.3 jit_solution(14303943591055082367)
XLA Ops:
  9.5 62.3 %reduce-scatter.13.cloned.1.call-done = f32[16,128]{1,0:T(8,128)} async-done(((f32[256,128]{1,0:T(8,128)}), f32[16,128]{1,0:T(8,128)}) %reduce-scatter.13.cloned.1.call-update) | async-done | bytes 8208 | tf_op jit(solution)/shard_map/reduce_scatter | solution.py:22
  73.2 4.7 all-to-all-start.2
  79.7 6.6 all-to-all-done.2
  87.0 27.2 %psum.56 = f32[128,64]{0,1:T(8,128)S(1)} all-reduce(f32[128,64]{0,1:T(8,128)S(1)} %convolution_bitcast_fusion.7), channel_id=1, replica_groups=mesh['leaf'=4,'row'=16,'col'=4] {'col'}, use_global_device_ids=true, to_apply=%region_3.4 | all-reduce | flops 8192 | bytes 65536 | tf_op jit(solution)/shard_map/psum | solution.py:33
  116.3 36.4 %reduce-scatter.11.cloned.1.call-done = f32[32,128]{1,0:T(8,128)} async-done(((f32[512,128]{1,0:T(8,128)}), f32[32,128]{1,0:T(8,128)}) %reduce-scatter.11.cloned.1.call-update) | async-done | bytes 16400 | tf_op jit(solution)/shard_map/reduce_scatter | solution.py:22
  157.4 5.1 all-to-all-start.1
  162.5 61.4 %reduce-scatter.15.cloned.1.call-done = f32[32,128]{1,0:T(8,128)} async-done(((f32[512,128]{1,0:T(8,128)}), f32[32,128]{1,0:T(8,128)}) %reduce-scatter.15.cloned.1.call-update) | async-done | bytes 16400 | tf_op jit(solution)/shard_map/reduce_scatter | solution.py:22
  234.7 7.6 all-to-all-done.3
  244.5 27.4 %psum.57 = f32[128,64]{0,1:T(8,128)S(1)} all-reduce(f32[128,64]{0,1:T(8,128)S(1)} %convolution_bitcast_fusion.6), channel_id=1, replica_groups=mesh['leaf'=4,'row'=16,'col'=4] {'col'}, use_global_device_ids=true, to_apply=%region_5.6 | all-reduce | flops 8192 | bytes 65536 | tf_op jit(solution)/shard_map/psum | solution.py:33
  274.5 33.5 %reduce-scatter.9.cloned.1.call-done = f32[64,128]{1,0:T(8,128)} async-done(((f32[1024,128]{1,0:T(8,128)}), f32[64,128]{1,0:T(8,128)}) %reduce-scatter.9.cloned.1.call-update) | async-done | bytes 32784 | tf_op jit(solution)/shard_map/reduce_scatter | solution.py:22
  322.4 57.9 %reduce-scatter.17.cloned.1.call-done = f32[64,128]{1,0:T(8,128)} async-done(((f32[1024,128]{1,0:T(8,128)}), f32[64,128]{1,0:T(8,128)}) %reduce-scatter.17.cloned.1.call-update) | async-done | bytes 32784 | tf_op jit(solution)/shard_map/reduce_scatter | solution.py:22
  389.1 17.0 %all_to_all.40 = f32[16,64,128]{2,1,0:T(8,128)S(1)} all-to-all(f32[16,64,128]{2,1,0:T(8,128)S(1)} %stack.20), channel_id=1, replica_groups=mesh['leaf'=4,'row'=16,'col'=4] {'row'}, dimensions={0} | all-to-all | bytes 1048576 | tf_op jit(solution)/shard_map/all_to_all | solution.py:27
  408.2 27.2 %psum.58 = f32[128,64]{0,1:T(8,128)S(1)} all-reduce(f32[128,64]{0,1:T(8,128)S(1)} %convolution_bitcast_fusion.5), channel_id=1, replica_groups=mesh['leaf'=4,'row'=16,'col'=4] {'col'}, use_global_device_ids=true, to_apply=%region_7.8 | all-reduce | flops 8192 | bytes 65536 | tf_op jit(solution)/shard_map/psum | solution.py:33
  437.5 56.2 %reduce-scatter.19.cloned.1.call-done = f32[64,128]{1,0:T(8,128)} async-done(((f32[1024,128]{1,0:T(8,128)}), f32[64,128]{1,0:T(8,128)}) %reduce-scatter.19.cloned.1.call-update) | async-done | bytes 32784 | tf_op jit(solution)/shard_map/reduce_scatter | solution.py:22
  507.4 11.8 %all-to-all-done.5 = f32[16,64,128]{2,1,0:T(8,128)S(1)} async-done(((f32[16,64,128]{2,1,0:T(8,128)}), f32[16,64,128]{2,1,0:T(8,128)S(1)}, u32[]{:S(2)}, u32[]{:S(2)}) %all-to-all-start.5) | async-done | bytes 524320 | tf_op jit(solution)/shard_map/all_to_all | solution.py:27
  522.5 28.2 %psum.60 = f32[128,64]{0,1:T(8,128)S(1)} all-reduce(f32[128,64]{0,1:T(8,128)S(1)} %bitcast.66), channel_id=1, replica_groups=mesh['leaf'=4,'row'=16,'col'=4] {'col'}, use_global_device_ids=true, to_apply=%region_10.11 | all-reduce | flops 8192 | bytes 65536 | tf_op jit(solution)/shard_map/psum | solution.py:37
  552.2 54.7 %reduce-scatter.21.cloned.1.call-done = f32[32,128]{1,0:T(8,128)} async-done(((f32[512,128]{1,0:T(8,128)}), f32[32,128]{1,0:T(8,128)}) %reduce-scatter.21.cloned.1.call-update) | async-done | bytes 16400 | tf_op jit(solution)/shard_map/reduce_scatter | solution.py:22
  611.6 5.0 all-to-all-start.6
  616.7 9.5 %all-to-all-done.6 = f32[16,32,128]{2,1,0:T(8,128)S(1)} async-done(((f32[16,32,128]{2,1,0:T(8,128)}), f32[16,32,128]{2,1,0:T(8,128)S(1)}, u32[]{:S(2)}, u32[]{:S(2)}) %all-to-all-start.6) | async-done | bytes 262176 | tf_op jit(solution)/shard_map/all_to_all | solution.py:27
  627.6 27.2 %psum.62 = f32[128,64]{0,1:T(8,128)S(1)} all-reduce(f32[128,64]{0,1:T(8,128)S(1)} %bitcast.67), channel_id=1, replica_groups=mesh['leaf'=4,'row'=16,'col'=4] {'col'}, use_global_device_ids=true, to_apply=%region_13.14 | all-reduce | flops 8192 | bytes 65536 | tf_op jit(solution)/shard_map/psum | solution.py:37
  656.0 54.2 %reduce-scatter.23.cloned.1.call-done = f32[16,128]{1,0:T(8,128)} async-done(((f32[256,128]{1,0:T(8,128)}), f32[16,128]{1,0:T(8,128)}) %reduce-scatter.23.cloned.1.call-update) | async-done | bytes 8208 | tf_op jit(solution)/shard_map/reduce_scatter | solution.py:22
  711.5 4.7 all-to-all-start.7
  718.0 6.7 all-to-all-done.7
  725.5 55.7 %all-reduce.6.cloned.1.call-done = (f32[128,64]{1,0:T(8,128)}, f32[128,64]{1,0:T(8,128)}, f32[128,64]{1,0:T(8,128)}) async-done(((f32[128,64]{1,0:T(8,128)}, f32[128,64]{1,0:T(8,128)}, f32[128,64]{1,0:T(8,128)}), (f32[128,64]{1,0:T(8,128)}, f32[128,64]{1,0:T(8,128)}, f32[128,64]{1,0:T(8,128)})) %all-reduce.6.cloned.1.call-update) | async-done | bytes 98320 | tf_op jit(solution)/shard_map/psum | solution.py:37
  (147 shorter events, 89.7 us)
Async XLA Ops:
  7.2 64.7 %reduce-scatter.13.cloned.1.call-start = ((), (), s32[]{:S(2)}) async-start(), calls=%async_computation.18 | async-start | bytes 139264 | tf_op jit(solution)/shard_map/reduce_scatter | solution.py:22
  73.2 13.1 %all-to-all-start.2 = ((f32[16,16,128]{2,1,0:T(8,128)}), f32[16,16,128]{2,1,0:T(8,128)S(1)}, u32[]{:S(2)}, u32[]{:S(2)}) async-start(f32[16,16,128]{2,1,0:T(8,128)} %stack.18), calls=%async_computation.5 | async-start | bytes 262144 | tf_op jit(solution)/shard_map/all_to_all | solution.py:27
  77.9 74.8 %reduce-scatter.11.cloned.1.call-start = ((), (), s32[]{:S(2)}) async-start(), calls=%async_computation.17 | async-start | bytes 278528 | tf_op jit(solution)/shard_map/reduce_scatter | solution.py:22
  79.6 144.2 %reduce-scatter.15.cloned.1.call-start = ((), (), s32[]{:S(2)}) async-start(), calls=%async_computation.19 | async-start | bytes 278528 | tf_op jit(solution)/shard_map/reduce_scatter | solution.py:22
  152.7 3.2 collective-permute-start.2
  157.4 70.4 %all-to-all-start.1 = ((f32[16,32,128]{2,1,0:T(8,128)}), f32[16,32,128]{2,1,0:T(8,128)S(1)}, u32[]{:S(2)}, u32[]{:S(2)}) async-start(f32[16,32,128]{2,1,0:T(8,128)} %stack.17), calls=%async_computation.3 | async-start | bytes 524288 | tf_op jit(solution)/shard_map/all_to_all | solution.py:27
  223.8 3.2 collective-permute-start.3
  228.5 13.8 %all-to-all-start.3 = ((f32[16,32,128]{2,1,0:T(8,128)}), f32[16,32,128]{2,1,0:T(8,128)}, u32[]{:S(2)}, u32[]{:S(2)}) async-start(f32[16,32,128]{2,1,0:T(8,128)} %stack.19), calls=%async_computation.7 | async-start | bytes 524288 | tf_op jit(solution)/shard_map/all_to_all | solution.py:27
  232.7 75.3 %reduce-scatter.9.cloned.1.call-start = ((), (), s32[]{:S(2)}) async-start(), calls=%async_computation.16 | async-start | bytes 557056 | tf_op jit(solution)/shard_map/reduce_scatter | solution.py:22
  234.6 145.6 %reduce-scatter.17.cloned.1.call-start = ((), (), s32[]{:S(2)}) async-start(), calls=%async_computation.20 | async-start | bytes 557056 | tf_op jit(solution)/shard_map/reduce_scatter | solution.py:22
  308.0 4.3 collective-permute-start
  313.0 4.3 collective-permute-start.1
  318.2 70.9 %all-to-all-start = ((f32[16,64,128]{2,1,0:T(8,128)}), f32[16,64,128]{2,1,0:T(8,128)S(1)}, u32[]{:S(2)}, u32[]{:S(2)}) async-start(f32[16,64,128]{2,1,0:T(8,128)} %stack.16), calls=%async_computation.1 | async-start | bytes 1048576 | tf_op jit(solution)/shard_map/all_to_all | solution.py:27
  322.3 171.3 %reduce-scatter.19.cloned.1.call-start = ((), (), s32[]{:S(2)}) async-start(), calls=%async_computation.21 | async-start | bytes 557056 | tf_op jit(solution)/shard_map/reduce_scatter | solution.py:22
  380.3 3.7 collective-permute-start.4
  384.7 4.3 collective-permute-start.5
  493.6 3.4 collective-permute-start.6
  497.8 4.3 collective-permute-start.7
  502.9 16.3 %all-to-all-start.5 = ((f32[16,64,128]{2,1,0:T(8,128)}), f32[16,64,128]{2,1,0:T(8,128)S(1)}, u32[]{:S(2)}, u32[]{:S(2)}) async-start(f32[16,64,128]{2,1,0:T(8,128)} %stack.21), calls=%async_computation.11 | async-start | bytes 1048576 | tf_op jit(solution)/shard_map/all_to_all | solution.py:27
  507.3 99.6 %reduce-scatter.21.cloned.1.call-start = ((), (), s32[]{:S(2)}) async-start(), calls=%async_computation.22 | async-start | bytes 278528 | tf_op jit(solution)/shard_map/reduce_scatter | solution.py:22
  611.6 14.7 %all-to-all-start.6 = ((f32[16,32,128]{2,1,0:T(8,128)}), f32[16,32,128]{2,1,0:T(8,128)S(1)}, u32[]{:S(2)}, u32[]{:S(2)}) async-start(f32[16,32,128]{2,1,0:T(8,128)} %stack.22), calls=%async_computation.13 | async-start | bytes 524288 | tf_op jit(solution)/shard_map/all_to_all | solution.py:27
  616.7 93.5 %reduce-scatter.23.cloned.1.call-start = ((), (), s32[]{:S(2)}) async-start(), calls=%async_computation.23 | async-start | bytes 139264 | tf_op jit(solution)/shard_map/reduce_scatter | solution.py:22
  711.5 13.2 %all-to-all-start.7 = ((f32[16,16,128]{2,1,0:T(8,128)}), f32[16,16,128]{2,1,0:T(8,128)S(1)}, u32[]{:S(2)}, u32[]{:S(2)}) async-start(f32[16,16,128]{2,1,0:T(8,128)} %stack.23), calls=%async_computation.15 | async-start | bytes 262144 | tf_op jit(solution)/shard_map/all_to_all | solution.py:27
  716.3 64.9 %all-reduce.6.cloned.1.call-start = ((), (), s32[]{:S(2)}) async-start(), calls=%async_computation.24 | async-start | bytes 393216 | tf_op jit(solution)/shard_map/psum | solution.py:37
  (14 other events, 899.1 us)
Sparse Core Ops, SparseCore 0:
  10.5 61.2 reduce-scatter.12
  81.3 71.3 reduce-scatter.10
  155.2 68.5 reduce-scatter.14
  235.9 72.0 reduce-scatter.8
  310.3 69.9 reduce-scatter.16
  437.6 55.9 reduce-scatter.18
  552.3 54.5 reduce-scatter.20
  656.1 53.9 reduce-scatter.22
  725.6 55.5 all-reduce.5
